TPU v7x, 256 devices: a whole 4x4x8 slice. The times are simulated.
256 devices in a mesh: grp: 2 (over core), ctx: 64 (over x, z_lo, y), hd: 2 (over z_hi).
Axes of the slice: x: 4, y: 4, z: 8 (z_hi: 2, z_lo: 4; z = z_hi * 4 + z_lo), core: 2. Of those that a mesh axis runs over, the one named last changes fastest.
Arguments:
- video_q: bfloat16 [8192, 24, 128], P(('ctx', 'hd'), 'grp'), may hold values from -6 to 6
- video_k: bfloat16 [8192, 24, 128], P(('ctx', 'hd'), 'grp'), may hold values from -6 to 6
- video_v: bfloat16 [8192, 24, 128], P(('ctx', 'hd'), 'grp'), may hold values from -6 to 6
- positions: int32 [3, 8192], P(None, ('ctx', 'hd')), may hold values from 0 to 31, as said below
- text_q: bfloat16 [256, 24, 128], P(None, ('grp', 'hd')), may hold values from -16 to 16
- text_k: bfloat16 [256, 24, 128], P(None, ('grp', 'hd')), may hold values from -16 to 16
- text_v: bfloat16 [256, 24, 128], P(None, ('grp', 'hd')), may hold values from -6 to 6
- text_count: int32 [1], replicated, may hold values from 64 to 256
Outputs:
- video_out: bfloat16 [8192, 24, 128], P(('ctx', 'hd'), 'grp')
- text_out: bfloat16 [256, 24, 128], P('ctx', ('grp', 'hd'))
Inputs may be any that keep to these rules, and one draw needn't show every extreme that they name: `positions`: column n holds the frame, row and column of video token n; the columns are distinct cells of a grid of 32 frames of 16 by 16 cells.
All inputs are finite; a program needn't handle non-finite values.
Results may differ from a plain program's by a relative error of at most 0.0073.
Values may be sent and summed in bfloat16 or wider, within the bound.
No kernel may reach another device: no remote copies, remote signals or barrier semaphores. Data moves between devices by JAX's collectives and lax.ppermute only.
A program may use at most 128 MiB of HBM per device.

v0:
```python
import math
import jax
import jax.numpy as jnp
from jax import lax
from jax.sharding import PartitionSpec as P

THETA = 256.0


def rotate(tokens_in, positions):
    head_dim = tokens_in.shape[-1]
    band_t = head_dim // 8
    band_h = (head_dim - band_t) // 2
    band_w = head_dim - band_t - band_h
    values = tokens_in.astype(jnp.float32)
    pieces = []
    offset = 0
    for axis_index, band_size in ((0, band_t), (1, band_h), (2, band_w)):
        half_size = band_size // 2
        frequency = THETA ** (-2.0 * jnp.arange(half_size, dtype=jnp.float32) / band_size)
        angles = positions[axis_index].astype(jnp.float32)[:, None] * frequency[None, :]
        cos_table = jnp.cos(angles)[:, None, :]
        sin_table = jnp.sin(angles)[:, None, :]
        lower_half = values[:, :, offset : offset + half_size]
        upper_half = values[:, :, offset + half_size : offset + band_size]
        pieces.append(lower_half * cos_table - upper_half * sin_table)
        pieces.append(upper_half * cos_table + lower_half * sin_table)
        offset += band_size
    return jnp.concatenate(pieces, axis=-1).astype(jnp.bfloat16)


def local(video_q, video_k, video_v, positions, text_q, text_k, text_v, text_count):
    rotated_q = rotate(video_q, positions)
    rotated_k = rotate(video_k, positions)
    queries_video, keys_video, values_video = (
        lax.all_to_all(rotated_q, "hd", split_axis=1, concat_axis=0, tiled=True),
        lax.all_to_all(rotated_k, "hd", split_axis=1, concat_axis=0, tiled=True),
        lax.all_to_all(video_v, "hd", split_axis=1, concat_axis=0, tiled=True),
    )
    cycle_size = lax.axis_size("ctx")
    text_share = text_q.shape[0] // cycle_size
    own_text = lax.dynamic_slice_in_dim(text_q, lax.axis_index("ctx") * text_share, text_share, 0)
    queries = jnp.concatenate([queries_video, own_text], axis=0)
    scale = 1.0 / math.sqrt(queries.shape[-1])
    text_live = jnp.arange(text_k.shape[0], dtype=jnp.int32) < text_count[0]
    scores = jnp.einsum("qhd,khd->qhk", queries, text_k, preferred_element_type=jnp.float32) * scale
    scores = jnp.where(text_live[None, None, :], scores, -jnp.inf)
    peak = jnp.max(scores, axis=2)
    probs = jnp.exp(scores - peak[..., None])
    total = jnp.sum(probs, axis=2)
    mixed = jnp.einsum(
        "qhk,khd->qhd", probs.astype(jnp.bfloat16), text_v, preferred_element_type=jnp.float32
    )
    keys_all, values_all = (
        lax.all_gather(keys_video, "ctx", axis=0, tiled=True),
        lax.all_gather(values_video, "ctx", axis=0, tiled=True),
    )
    piece_scores = (
        jnp.einsum("qhd,khd->qhk", queries, keys_all, preferred_element_type=jnp.float32) * scale
    )
    new_peak = jnp.maximum(peak, jnp.max(piece_scores, axis=2))
    factor = jnp.exp(peak - new_peak)
    piece_probs = jnp.exp(piece_scores - new_peak[..., None])
    new_total = total * factor + jnp.sum(piece_probs, axis=2)
    new_mixed = mixed * factor[..., None] + jnp.einsum(
        "qhk,khd->qhd",
        piece_probs.astype(jnp.bfloat16),
        values_all,
        preferred_element_type=jnp.float32,
    )
    attended = (new_mixed / new_total[..., None]).astype(jnp.bfloat16)
    video_rows = queries_video.shape[0]
    video_heads = attended[:video_rows]
    text_out = attended[video_rows:]
    video_out = lax.all_to_all(video_heads, "hd", split_axis=0, concat_axis=1, tiled=True)
    return (video_out, text_out)


def solution(mesh):
    return jax.shard_map(
        local,
        mesh=mesh,
        in_specs=(
            P(("ctx", "hd"), "grp", None),
            P(("ctx", "hd"), "grp", None),
            P(("ctx", "hd"), "grp", None),
            P(None, ("ctx", "hd")),
            P(None, ("grp", "hd"), None),
            P(None, ("grp", "hd"), None),
            P(None, ("grp", "hd"), None),
            P(),
        ),
        out_specs=(P(("ctx", "hd"), "grp", None), P("ctx", ("grp", "hd"), None)),
        check_vma=False,
    )
```

profile of v0, /device:TPU:16, one launch (start us, length us, event | category | flops | bytes accessed | tf_op | source)
XLA Modules:
  0.0 811.1 jit_solution(17973969847977759047)
XLA Ops:
  7.3 0.8 convert_bitcast_fusion
  8.1 1.0 convert_element_type.50
  9.0 0.1 multiply_cosine_fusion.2
  9.1 0.1 copy.19
  9.2 0.1 copy.20
  9.3 1.0 convert_element_type.58
  10.3 0.3 multiply_cosine_fusion
  10.6 0.4 add_convert_fusion.5
  10.9 0.5 add_convert_fusion
  11.4 0.6 concatenate.13
  12.0 18.1 %all_to_all.72 = bf16[64,12,128]{2,0,1:T(8,128)(2,1)S(1)} all-to-all(bf16[64,12,128]{2,0,1:T(8,128)(2,1)S(1)} %concatenate.13), channel_id=1, replica_groups=mesh['grp'=2,'ctx'=64,'hd'=2] {'hd'}, dimensions={1} | all-to-all | bytes 393216 | tf_op jit(solution)/shard_map/all_to_all | solution.py:37
  30.1 0.7 copy.22
  30.9 12.4 %all_to_all.73 = bf16[64,12,128]{2,0,1:T(8,128)(2,1)S(1)} all-to-all(bf16[64,12,128]{2,0,1:T(8,128)(2,1)} %param.10), channel_id=1, replica_groups=mesh['grp'=2,'ctx'=64,'hd'=2] {'hd'}, dimensions={1} | all-to-all | bytes 393216 | tf_op jit(solution)/shard_map/all_to_all | solution.py:38
  43.3 0.7 copy.23
  44.0 0.5 add_convert_fusion.3
  44.5 1.2 concatenate.11
  45.7 3.4 all-to-all-start
  49.8 0.7 constant_dynamic-slice_fusion
  50.5 8.4 %all-to-all-done = bf16[64,12,128]{2,0,1:T(8,128)(2,1)S(1)} async-done(((bf16[64,12,128]{2,0,1:T(8,128)(2,1)}), bf16[64,12,128]{2,0,1:T(8,128)(2,1)S(1)}, u32[]{:S(2)}, u32[]{:S(2)}) %all-to-all-start) | async-done | bytes 196640 | tf_op jit(solution)/shard_map/all_to_all | solution.py:36
  58.9 0.5 fusion.24
  59.5 0.5 fusion.16
  59.9 338.1 %all-gather.3.cloned.1.call-done = bf16[8192,6,128]{2,0,1:T(8,128)(2,1)} async-done(((bf16[128,6,128]{2,0,1:T(8,128)(2,1)}), bf16[8192,6,128]{2,0,1:T(8,128)(2,1)}) %all-gather.3.cloned.1.call-update) | async-done | bytes 12582928 | tf_op jit(solution)/shard_map/all_gather | solution.py:55
  398.1 16.2 %bitcast_reduce_fusion = (f32[132,6]{0,1:T(8,128)S(1)}, f32[6,8192,132]{1,2,0:T(8,128)}) fusion(bf16[8192,6,128]{2,0,1:T(8,128)(2,1)} %all-gather.3.cloned.1.call-done, bf16[4,6,128]{2,0,1:T(4,128)(2,1)S(1)} %constant_dynamic-slice_fusion, bf16[128,6,128]{2,0,1:T(8,128)(2,1)S(1)} %bitcast.55), kind=kOutput, calls=%fused_computation.1 | convolution fusion | flops 1674325248 | bytes 38741088 | tf_op jit(solution)/shard_map/qhd,khd->qhk/dot_general | solution.py:59
  414.3 11.4 %fusion.1 = f32[132,6]{0,1:T(8,128)S(1)} fusion(f32[6,8192,132]{1,2,0:T(8,128)} %get-tuple-element.36, f32[132,6]{0,1:T(8,128)S(1)} %max.13), kind=kLoop, calls=%fused_computation.3 | loop fusion | flops 19463400 | bytes 25958592 | tf_op jit(solution)/shard_map/reduce_sum | solution.py:64
  425.8 348.9 %all-gather.5.cloned.1.call-done = bf16[8192,6,128]{2,0,1:T(8,128)(2,1)} async-done(((bf16[128,6,128]{2,0,1:T(8,128)(2,1)}), bf16[8192,6,128]{2,0,1:T(8,128)(2,1)}) %all-gather.5.cloned.1.call-update) | async-done | bytes 12582928 | tf_op jit(solution)/shard_map/all_gather | solution.py:56
  774.6 15.2 %fusion.12 = f32[132,6,128]{2,0,1:T(8,128)S(1)} fusion(bf16[8192,6,128]{2,0,1:T(8,128)(2,1)} %all-gather.5.cloned.1.call-done, f32[6,8192,132]{1,2,0:T(8,128)} %get-tuple-element.36, f32[132,6]{0,1:T(8,128)S(1)} %max.13), kind=kOutput, calls=%fused_computation.15 | convolution fusion | flops 1680408576 | bytes 38943840 | tf_op jit(solution)/shard_map/qhk,khd->qhd/dot_general | solution.py:65
  789.8 0.4 fusion.15
  790.2 0.8 copy.24
  791.1 3.4 all-to-all-start.3
  794.5 0.6 slice.84
  795.1 8.5 %all-to-all-done.3 = bf16[128,6,128]{2,1,0:T(8,128)(2,1)S(1)} async-done(((bf16[128,6,128]{2,1,0:T(8,128)(2,1)}), bf16[128,6,128]{2,1,0:T(8,128)(2,1)S(1)}, u32[]{:S(2)}, u32[]{:S(2)}) %all-to-all-start.3) | async-done | bytes 196640 | tf_op jit(solution)/shard_map/all_to_all | solution.py:75
  803.6 0.7 copy.25
  (15 shorter events, 0.2 us)
Async XLA Ops:
  7.2 51.8 %copy-start = (bf16[256,6,128]{2,0,1:T(8,128)(2,1)S(1)}, bf16[256,6,128]{2,0,1:T(8,128)(2,1)}, u32[]{:S(2)}) copy-start(bf16[256,6,128]{2,0,1:T(8,128)(2,1)} %param.13) | copy-start | bytes 1179652
  7.2 390.9 %all-gather.3.cloned.1.call-start = ((), (), s32[]{:S(2)}) async-start(), calls=%async_computation.4 | async-start | bytes 12779520 | tf_op jit(solution)/shard_map/all_gather | solution.py:55
  30.8 743.8 %all-gather.5.cloned.1.call-start = ((), (), s32[]{:S(2)}) async-start(), calls=%async_computation.5 | async-start | bytes 12779520 | tf_op jit(solution)/shard_map/all_gather | solution.py:56
  45.7 13.2 %all-to-all-start = ((bf16[64,12,128]{2,0,1:T(8,128)(2,1)}), bf16[64,12,128]{2,0,1:T(8,128)(2,1)S(1)}, u32[]{:S(2)}, u32[]{:S(2)}) async-start(bf16[64,12,128]{2,0,1:T(8,128)(2,1)} %concatenate.11), calls=%async_computation | async-start | bytes 393216 | tf_op jit(solution)/shard_map/all_to_all | solution.py:36
  414.3 375.5 %copy-start.1 = (bf16[256,6,128]{2,0,1:T(8,128)(2,1)S(1)}, bf16[256,6,128]{2,0,1:T(8,128)(2,1)}, u32[]{:S(2)}) copy-start(bf16[256,6,128]{2,0,1:T(8,128)(2,1)} %param.14) | copy-start | bytes 1179652
  791.1 12.5 %all-to-all-start.3 = ((bf16[128,6,128]{2,1,0:T(8,128)(2,1)}), bf16[128,6,128]{2,1,0:T(8,128)(2,1)S(1)}, u32[]{:S(2)}, u32[]{:S(2)}) async-start(bf16[128,6,128]{2,1,0:T(8,128)(2,1)} %copy.24), calls=%async_computation.3 | async-start | bytes 524288 | tf_op jit(solution)/shard_map/all_to_all | solution.py:75
Sparse Core Ops, SparseCore 0:
  31.0 367.0 all-gather.2
  400.4 374.1 all-gather.4
where the time goes:
time: 812 us; the launch traced here: 811 us
  waiting for transfers between devices  704 us (87%)
  matrix products  32.4 us (4%)
  blocking collectives  30.5 us (4%)
  other arithmetic  16.3 us (2%)
  between operations  14.8 us (2%)
    all_gather x1, waiting for transfers between devices, local(): lax.all_gather(values_video, 'ctx', axis=0, tiled=True)  349 us
    all_gather x1, waiting for transfers between devices, local(): lax.all_gather(keys_video, 'ctx', axis=0, tiled=True)  338 us
    all_to_all x1, blocking collectives, local(): lax.all_to_all(rotated_k, 'hd', split_axis=1, concat_axis=0, tiled=True)  18.1 us
    dot_general x1, matrix products, local(): jnp.einsum('qhd,khd->qhk', queries, keys_all, preferred_element_type=jnp....  16.2 us
  transfers between devices with their start and end apart: 4, of which 4 were waited for; matrix products, arithmetic and copies ran while one was open for 4% of the time, Pallas kernels for 0%

commit v1 on v0

--- a/solution.py
+++ b/solution.py
@@ -53,7 +53,9 @@
     )
     keys_all, values_all = (
         lax.all_gather(keys_video, "ctx", axis=0, tiled=True),
-        lax.all_gather(values_video, "ctx", axis=0, tiled=True),
+        jnp.concatenate(
+            lax.all_to_all(jnp.stack([values_video] * lax.axis_size("ctx")), "ctx", 0, 0), axis=0
+        ),
     )
     piece_scores = (
         jnp.einsum("qhd,khd->qhk", queries, keys_all, preferred_element_type=jnp.float32) * scale

time: 812 us -> 592 us (0.73)
  waiting for transfers between devices: 704 us -> 458 us
  local copies, waits for them, and re-layouts: 6.24 us -> 24.1 us
  starting transfers between devices: 6.95 us -> 22.2 us
  blocking collectives: 30.5 us -> 18.1 us
    all_gather x1 -> x0, waiting for transfers between devices: 349 us -> none  [local(): lax.all_gather(values_video, 'ctx', axis=0, tiled=True)]
    all_gather x1, waiting for transfers between devices: 338 us -> 433 us  [local(): lax.all_gather(keys_video, 'ctx', axis=0, tiled=True)]
    all_to_all x0 -> x2, starting transfers between devices: none -> 14.9 us  [the longest x1 11.5 us: local(): lax.all_to_all(jnp.stack([values_video] * lax.axis_size('ctx')), 'ctx', 0...]
    all_to_all x1 -> x0, blocking collectives: 12.4 us -> none  [local(): lax.all_to_all(video_v, 'hd', split_axis=1, concat_axis=0, tiled=True)]
    all_to_all x0 -> x1, local copies, waits for them, and re-layouts: none -> 10.8 us  [local(): lax.all_to_all(jnp.stack([values_video] * lax.axis_size('ctx')), 'ctx', 0...]
  transfers between devices with their start and end apart: 4 -> 5, of which waited for: 4 -> 4; matrix products, arithmetic and copies ran while one was open for 4% -> 7% of each run, Pallas kernels for 0% -> 0%
where the time goes in v1:
time: 592 us; the launch traced here: 586 us
  waiting for transfers between devices  458 us (77%)
  matrix products  32.3 us (5%)
  local copies, waits for them, and re-layouts  24.1 us (4%)
  starting transfers between devices  22.2 us (4%)
  blocking collectives  18.1 us (3%)
  other arithmetic  16.2 us (3%)
  between operations  14.9 us (3%)
    all_gather x1, waiting for transfers between devices, local(): lax.all_gather(keys_video, 'ctx', axis=0, tiled=True)  433 us
    all_to_all x1, blocking collectives, local(): lax.all_to_all(rotated_k, 'hd', split_axis=1, concat_axis=0, tiled=True)  18.1 us
    dot_general x1, matrix products, local(): jnp.einsum('qhd,khd->qhk', queries, keys_all, preferred_element_type=jnp....  16.2 us
    dot_general x1, matrix products, local(): jnp.einsum('qhk,khd->qhd', piece_probs.astype(jnp.bfloat16), values_all,...  15.2 us
  transfers between devices with their start and end apart: 5, of which 4 were waited for; matrix products, arithmetic and copies ran while one was open for 7% of the time, Pallas kernels for 0%

profile of v1, /device:TPU:16, one launch (start us, length us, event | category | flops | bytes accessed | tf_op | source)
XLA Modules:
  0.0 586.1 jit_solution(16272584318323827168)
XLA Ops:
  7.3 1.0 convert_element_type.50
  8.3 0.8 convert_bitcast_fusion
  9.1 0.1 multiply_cosine_fusion.2
  9.3 1.0 convert_element_type.58
  10.3 0.3 multiply_cosine_fusion
  10.6 0.4 add_convert_fusion.5
  11.0 0.5 add_convert_fusion
  11.5 0.6 concatenate.13
  12.1 18.1 %all_to_all.74 = bf16[64,12,128]{2,0,1:T(8,128)(2,1)S(1)} all-to-all(bf16[64,12,128]{2,0,1:T(8,128)(2,1)S(1)} %concatenate.13), channel_id=1, replica_groups=mesh['grp'=2,'ctx'=64,'hd'=2] {'hd'}, dimensions={1} | all-to-all | bytes 393216 | tf_op jit(solution)/shard_map/all_to_all | solution.py:37
  30.2 0.7 copy.29
  30.9 3.4 all-to-all-start.2
  34.3 0.5 add_convert_fusion.3
  34.8 1.2 concatenate.11
  36.0 7.3 %all-to-all-done.2 = bf16[64,12,128]{2,0,1:T(8,128)(2,1)S(1)} async-done(((bf16[64,12,128]{2,0,1:T(8,128)(2,1)}), bf16[64,12,128]{2,0,1:T(8,128)(2,1)S(1)}, u32[]{:S(2)}, u32[]{:S(2)}) %all-to-all-start.2) | async-done | bytes 196640 | tf_op jit(solution)/shard_map/all_to_all | solution.py:38
  43.3 3.4 all-to-all-start
  46.8 9.8 %all-to-all-done = bf16[64,12,128]{2,0,1:T(8,128)(2,1)S(1)} async-done(((bf16[64,12,128]{2,0,1:T(8,128)(2,1)}), bf16[64,12,128]{2,0,1:T(8,128)(2,1)S(1)}, u32[]{:S(2)}, u32[]{:S(2)}) %all-to-all-start) | async-done | bytes 196640 | tf_op jit(solution)/shard_map/all_to_all | solution.py:36
  56.5 7.8 %stack.5 = bf16[64,128,6,128]{3,1,2,0:T(8,128)(2,1)} broadcast(bf16[128,6,128]{2,0,1:T(8,128)(2,1)S(1)} %bitcast.63), dimensions={1,2,3} | broadcast | bytes 12779520 | tf_op jit(solution)/shard_map/stack | solution.py:57
  64.3 11.5 %all-to-all-start.3 = ((bf16[64,128,6,128]{3,1,2,0:T(8,128)(2,1)}), bf16[64,128,6,128]{3,1,2,0:T(8,128)(2,1)}, u32[]{:S(2)}, u32[]{:S(2)}) async-start(bf16[64,128,6,128]{3,1,2,0:T(8,128)(2,1)} %stack.5), calls=%async_computation.3 | async-start | bytes 25165824 | tf_op jit(solution)/shard_map/all_to_all | solution.py:57
  76.4 0.7 constant_dynamic-slice_fusion
  77.2 0.5 fusion.24
  77.7 0.5 fusion.16
  78.2 432.6 %all-gather.2.cloned.1.call-done = bf16[8192,6,128]{2,0,1:T(8,128)(2,1)} async-done(((bf16[128,6,128]{2,0,1:T(8,128)(2,1)}), bf16[8192,6,128]{2,0,1:T(8,128)(2,1)}) %all-gather.2.cloned.1.call-update) | async-done | bytes 12582928 | tf_op jit(solution)/shard_map/all_gather | solution.py:55
  510.8 16.2 %bitcast_reduce_fusion = (f32[132,6]{0,1:T(8,128)S(1)}, f32[6,8192,132]{1,2,0:T(8,128)}) fusion(bf16[8192,6,128]{2,0,1:T(8,128)(2,1)} %all-gather.2.cloned.1.call-done, bf16[4,6,128]{2,0,1:T(4,128)(2,1)S(1)} %constant_dynamic-slice_fusion, bf16[128,6,128]{2,0,1:T(8,128)(2,1)S(1)} %bitcast.57), kind=kOutput, calls=%fused_computation.1 | convolution fusion | flops 1674325248 | bytes 38741088 | tf_op jit(solution)/shard_map/qhd,khd->qhk/dot_general | solution.py:61
  527.0 11.3 %fusion.1 = f32[132,6]{0,1:T(8,128)S(1)} fusion(f32[6,8192,132]{1,2,0:T(8,128)} %get-tuple-element.36, f32[132,6]{0,1:T(8,128)S(1)} %max.13), kind=kLoop, calls=%fused_computation.3 | loop fusion | flops 19463400 | bytes 25958592 | tf_op jit(solution)/shard_map/reduce_sum | solution.py:66
  538.4 10.8 %copy.31 = bf16[64,128,6,128]{3,1,0,2:T(8,128)(2,1)} copy(bf16[64,128,6,128]{3,1,2,0:T(8,128)(2,1)} %all-to-all-done.3) | data formatting | bytes 25165824 | tf_op jit(solution)/shard_map/all_to_all | solution.py:57
  549.1 15.2 %fusion.12 = f32[132,6,128]{2,0,1:T(8,128)S(1)} fusion(bf16[8192,6,128]{2,0,1:T(8,128)(2,1)} %bitcast.55, f32[6,8192,132]{1,2,0:T(8,128)} %get-tuple-element.36, f32[132,6]{0,1:T(8,128)S(1)} %max.13), kind=kOutput, calls=%fused_computation.15 | convolution fusion | flops 1680408576 | bytes 38943840 | tf_op jit(solution)/shard_map/qhk,khd->qhd/dot_general | solution.py:67
  564.3 0.4 fusion.15
  564.8 0.8 copy.32
  565.6 3.8 all-to-all-start.4
  569.4 0.6 slice.84
  570.0 8.5 %all-to-all-done.4 = bf16[128,6,128]{2,1,0:T(8,128)(2,1)S(1)} async-done(((bf16[128,6,128]{2,1,0:T(8,128)(2,1)}), bf16[128,6,128]{2,1,0:T(8,128)(2,1)S(1)}, u32[]{:S(2)}, u32[]{:S(2)}) %all-to-all-start.4) | async-done | bytes 196640 | tf_op jit(solution)/shard_map/all_to_all | solution.py:77
  578.5 0.7 copy.33
  (19 shorter events, 0.3 us)
Async XLA Ops:
  7.2 70.0 %copy-start = (bf16[256,6,128]{2,0,1:T(8,128)(2,1)S(1)}, bf16[256,6,128]{2,0,1:T(8,128)(2,1)}, u32[]{:S(2)}) copy-start(bf16[256,6,128]{2,0,1:T(8,128)(2,1)} %param.13) | copy-start | bytes 1179652
  7.2 503.6 %all-gather.2.cloned.1.call-start = ((), (), s32[]{:S(2)}) async-start(), calls=%async_computation.5 | async-start | bytes 12779520 | tf_op jit(solution)/shard_map/all_gather | solution.py:55
  30.9 12.4 %all-to-all-start.2 = ((bf16[64,12,128]{2,0,1:T(8,128)(2,1)}), bf16[64,12,128]{2,0,1:T(8,128)(2,1)S(1)}, u32[]{:S(2)}, u32[]{:S(2)}) async-start(bf16[64,12,128]{2,0,1:T(8,128)(2,1)} %param.10), calls=%async_computation.2 | async-start | bytes 393216 | tf_op jit(solution)/shard_map/all_to_all | solution.py:38
  43.3 13.2 %all-to-all-start = ((bf16[64,12,128]{2,0,1:T(8,128)(2,1)}), bf16[64,12,128]{2,0,1:T(8,128)(2,1)S(1)}, u32[]{:S(2)}, u32[]{:S(2)}) async-start(bf16[64,12,128]{2,0,1:T(8,128)(2,1)} %concatenate.11), calls=%async_computation | async-start | bytes 393216 | tf_op jit(solution)/shard_map/all_to_all | solution.py:36
  64.3 474.1 %all-to-all-start.3 = ((bf16[64,128,6,128]{3,1,2,0:T(8,128)(2,1)}), bf16[64,128,6,128]{3,1,2,0:T(8,128)(2,1)}, u32[]{:S(2)}, u32[]{:S(2)}) async-start(bf16[64,128,6,128]{3,1,2,0:T(8,128)(2,1)} %stack.5), calls=%async_computation.3 | async-start | bytes 25165824 | tf_op jit(solution)/shard_map/all_to_all | solution.py:57
  538.3 26.0 %copy-start.2 = (bf16[256,6,128]{2,0,1:T(8,128)(2,1)S(1)}, bf16[256,6,128]{2,0,1:T(8,128)(2,1)}, u32[]{:S(2)}) copy-start(bf16[256,6,128]{2,0,1:T(8,128)(2,1)} %param.14) | copy-start | bytes 1179652
  538.3 40.9 %copy-start.1 = (bf16[256,6,128]{2,0,1:T(8,128)(2,1)S(1)}, bf16[256,6,128]{2,0,1:T(8,128)(2,1)}, u32[]{:S(2)}) copy-start(bf16[256,6,128]{2,0,1:T(8,128)(2,1)} %param.13) | copy-start | bytes 1179652
  565.6 12.9 %all-to-all-start.4 = ((bf16[128,6,128]{2,1,0:T(8,128)(2,1)}), bf16[128,6,128]{2,1,0:T(8,128)(2,1)S(1)}, u32[]{:S(2)}, u32[]{:S(2)}) async-start(bf16[128,6,128]{2,1,0:T(8,128)(2,1)} %copy.32), calls=%async_computation.4 | async-start | bytes 524288 | tf_op jit(solution)/shard_map/all_to_all | solution.py:77
Sparse Core Ops, SparseCore 0:
  31.0 479.7 all-gather.1
